TPU v7x, 32 devices: a whole 2x2x4 slice. The times are simulated.
32 devices in a mesh: groups: 2 (over y), row: 8 (over z, x), col: 2 (over core).
Axes of the slice: x: 2, y: 2, z: 4, core: 2. Of those that a mesh axis runs over, the one named last changes fastest.
Arguments:
- probes: float32 [16, 16384], P(None, ('groups', 'row', 'col')), parts along dimension 1, may hold values from -23 to 30
- tiles: bfloat16 [1024, 256, 256], P(('groups', 'row', 'col')), parts along dimension 0, may hold values from -0.004895934 to 0.00511353114
- tile_rows: int32 [1024], P(('groups', 'row', 'col')), parts along dimension 0, may hold values from 0 to 31, as said below
- tile_cols: int32 [1024], P(('groups', 'row', 'col')), parts along dimension 0, may hold values from 0 to 31, as said below
- counts: int32 [1024], P(('groups', 'row', 'col')), parts along dimension 0, may hold values from 0 to 256, as said below
- diag_tiles: bfloat16 [64, 256, 256], P(('groups', 'row', 'col')), parts along dimension 0, as said below
Outputs:
- solution: float32 [16, 16384], P(None, ('groups', 'row', 'col')), parts along dimension 1
- residual: float32 [16, 16384], P(None, ('groups', 'row', 'col')), parts along dimension 1
There are 2 independent parts, one for each index of `groups`. A program takes and returns all parts, laid end to end along the dimension named above; each array names one. Nothing has to cross between parts.
Inputs may be any that keep to these rules, and one draw needn't show every extreme that they name: `tile_rows`: the device at index r of row and c of col holds the 32 slots starting at (2 r + c) * 32; their tile rows lie in 2 r * 2 to 2 r * 2 + 2 * 2 - 1. `tile_cols`: A slot's tile column j has (j // 2) % 2 equal to its device's index c of col; where counts is above zero, j exceeds the slot's tile row, and no pair of tile row and column appears twice. Slots with counts above zero come first among a device's slots and zeros follow; some device has all 32 slots above zero. `diag_tiles`: every tile is symmetric.
All inputs are finite; a program needn't handle non-finite values.
Results may differ from a plain program's by a relative error of at most 0.012.
The roundings to bfloat16 on the way count: a program that leaves them out, or rounds other values in their place, can miss the bound.
Values may be sent and summed in bfloat16 or wider, within the bound.
A program may use at most 64 MiB of HBM per device.

v0:
```python
import jax
import jax.numpy as jnp
from jax import lax
from jax.sharding import PartitionSpec as P

ITERS = 2


def gram_matrix(left, right):
    return jnp.dot(left, right.T, precision=lax.Precision.HIGHEST)


def small_solve(matrix, rhs):
    lower = jnp.linalg.cholesky(matrix)
    return jax.scipy.linalg.cho_solve((lower, True), rhs)


def row_total(slab_sums):
    return lax.psum_scatter(slab_sums, "row", scatter_dimension=1, tiled=True)


def local(probes, tiles, tile_rows, tile_cols, counts, diag_tiles):
    probe_count, segment_len = probes.shape
    per_segment, tile_size = (diag_tiles.shape[0], diag_tiles.shape[1])
    band_tiles = 2 * per_segment
    row_place = tile_rows % band_tiles
    col_place = tile_cols // band_tiles * per_segment + tile_cols % per_segment
    live_mask = (jnp.arange(tile_size)[None, :] < counts[:, None]).astype(jnp.bfloat16)
    solution = jnp.zeros_like(probes)
    residual = probes
    direction = probes
    squares = lax.psum(gram_matrix(residual, residual), ("row", "col"))
    for iteration in range(ITERS):
        rounded = direction.astype(jnp.bfloat16)
        band_vec = lax.all_gather(rounded, "col", axis=1, tiled=True).reshape(
            probe_count, band_tiles, tile_size
        )
        slab_flat = lax.all_gather(rounded, "row", axis=1, tiled=True)
        slab_tiles = slab_flat.shape[1] // tile_size
        slab_vec = slab_flat.reshape(probe_count, slab_tiles, tile_size)
        own_vec = rounded.reshape(probe_count, per_segment, tile_size)
        diag_part = jnp.einsum(
            "pta,tab->ptb", own_vec, diag_tiles, preferred_element_type=jnp.float32
        )
        src_rows = band_vec[:, row_place, :] * live_mask[None]
        src_cols = slab_vec[:, col_place, :]
        to_cols = jnp.einsum("pga,gab->pgb", src_rows, tiles, preferred_element_type=jnp.float32)
        to_rows = jnp.einsum("pgb,gab->pga", src_cols, tiles, preferred_element_type=jnp.float32)
        to_rows = to_rows * live_mask[None].astype(jnp.float32)
        band_part = (
            jnp.zeros((probe_count, band_tiles, tile_size), jnp.float32)
            .at[:, row_place, :]
            .add(to_rows)
        )
        slab_part = (
            jnp.zeros((probe_count, slab_tiles, tile_size), jnp.float32)
            .at[:, col_place, :]
            .add(to_cols)
        )
        slab_sums = slab_part.reshape(probe_count, slab_tiles * tile_size)
        slab_total = row_total(slab_sums)
        band_total = lax.psum_scatter(
            band_part.reshape(probe_count, band_tiles * tile_size).astype(jnp.bfloat16),
            "col",
            scatter_dimension=1,
            tiled=True,
        ).astype(jnp.float32)
        result = slab_total + band_total
        mapped = result + diag_part.reshape(probe_count, segment_len)
        curvature = lax.psum(gram_matrix(direction, mapped), ("row", "col"))
        step_size = small_solve(curvature, squares)
        solution = solution + jnp.dot(step_size.T, direction, precision=lax.Precision.HIGHEST)
        residual = residual - jnp.dot(step_size.T, mapped, precision=lax.Precision.HIGHEST)
        renewed = lax.psum(gram_matrix(residual, residual), ("row", "col"))
        blend = small_solve(squares, renewed)
        direction = residual + jnp.dot(blend.T, direction, precision=lax.Precision.HIGHEST)
        squares = renewed
    return (solution, residual)


def solution(mesh):
    in_specs = (
        P(None, ("groups", "row", "col")),
        P(("groups", "row", "col"), None, None),
        P(("groups", "row", "col")),
        P(("groups", "row", "col")),
        P(("groups", "row", "col")),
        P(("groups", "row", "col"), None, None),
    )
    out_specs = (P(None, ("groups", "row", "col")), P(None, ("groups", "row", "col")))
    return jax.shard_map(local, mesh=mesh, in_specs=in_specs, out_specs=out_specs, check_vma=False)
```

profile of v0, /device:TPU:0, one launch (start us, length us, event | category | flops | bytes accessed | tf_op | source)
XLA Modules:
  0.0 376.6 jit_solution(1964738034291137668)
XLA Ops:
  10.1 32.3 %all_gather.13 = bf16[16,4096]{1,0:T(8,128)(2,1)S(1)} all-gather(bf16[16,512]{1,0:T(8,128)(2,1)S(1)} %convert_element_type.43), channel_id=1, replica_groups=mesh['groups'=2,'row'=8,'col'=2] {'row'}, dimensions={1}, use_global_device_ids=true | all-gather | bytes 147456 | tf_op jit(solution)/shard_map/all_gather | solution.py:38
  43.0 3.4 convolution_multiply_fusion.1
  46.4 1.9 scatter_fusion.1
  49.0 1.8 all_gather.12
  51.4 2.8 fusion.4
  54.3 1.9 scatter_fusion
  57.4 65.8 %reduce-scatter.5.cloned.1.call-done = f32[16,512]{1,0:T(8,128)} async-done(((f32[16,4096]{1,0:T(8,128)}), f32[16,512]{1,0:T(8,128)}) %reduce-scatter.5.cloned.1.call-update) | async-done | bytes 32784 | tf_op jit(solution)/shard_map/reduce_scatter | solution.py:19
  124.1 57.7 %all-reduce = (f32[16,16]{0,1:T(8,128)S(1)}, f32[16,16]{0,1:T(8,128)S(1)}) all-reduce(f32[16,16]{0,1:T(8,128)S(1)} %fusion.38, f32[16,16]{0,1:T(8,128)S(1)} %convolution_bitcast_fusion.2), channel_id=1, replica_groups=mesh['groups'=2,'row'=8,'col'=2] {'row','col'}, use_global_device_ids=true, to_apply=%region_7.9 | all-reduce | flops 512 | bytes 4096 | tf_op jit(solution)/shard_map/psum | solution.py:32
  181.9 1.5 cholesky.70
  184.7 1.2 custom-call.10
  185.9 1.5 cholesky.59
  188.7 1.2 custom-call.9
  191.5 30.0 %psum.30 = f32[16,16]{1,0:T(8,128)S(1)} all-reduce(f32[16,16]{1,0:T(8,128)S(1)} %fusion.40), channel_id=1, replica_groups=mesh['groups'=2,'row'=8,'col'=2] {'row','col'}, use_global_device_ids=true, to_apply=%region_8.11 | all-reduce | flops 256 | bytes 2048 | tf_op jit(solution)/shard_map/psum | solution.py:74
  222.1 1.8 all_gather.14
  223.9 30.6 %all_gather.15 = bf16[16,4096]{1,0:T(8,128)(2,1)S(1)} all-gather(bf16[16,512]{1,0:T(8,128)(2,1)S(1)} %get-tuple-element.8), channel_id=1, replica_groups=mesh['groups'=2,'row'=8,'col'=2] {'row'}, dimensions={1}, use_global_device_ids=true | all-gather | bytes 147456 | tf_op jit(solution)/shard_map/all_gather | solution.py:38
  255.7 3.4 convolution_multiply_fusion
  259.1 1.9 scatter_fusion.3
  261.7 2.8 fusion.1
  264.5 1.9 scatter_fusion.2
  267.5 64.5 %reduce-scatter.9.cloned.1.call-done = f32[16,512]{1,0:T(8,128)} async-done(((f32[16,4096]{1,0:T(8,128)}), f32[16,512]{1,0:T(8,128)}) %reduce-scatter.9.cloned.1.call-update) | async-done | bytes 32784 | tf_op jit(solution)/shard_map/reduce_scatter | solution.py:19
  333.0 30.2 %psum.31 = f32[16,16]{0,1:T(8,128)S(1)} all-reduce(f32[16,16]{0,1:T(8,128)S(1)} %fusion.33), channel_id=1, replica_groups=mesh['groups'=2,'row'=8,'col'=2] {'row','col'}, use_global_device_ids=true, to_apply=%region_13.16 | all-reduce | flops 256 | bytes 2048 | tf_op jit(solution)/shard_map/psum | solution.py:70
  363.2 1.5 cholesky.81
  366.0 1.2 custom-call.11
  368.4 1.6 convolution_subtract_fusion
  (70 shorter events, 18.3 us)
Async XLA Ops:
  7.2 49.8 %copy-start = (bf16[2,256,256]{2,1,0:T(8,128)(2,1)S(1)}, bf16[2,256,256]{2,1,0:T(8,128)(2,1)}, u32[]{:S(2)}) copy-start(bf16[2,256,256]{2,1,0:T(8,128)(2,1)} %param.14) | copy-start | bytes 786436
  7.2 50.3 %reduce-scatter.7.cloned.1.call-start = ((), (), s32[]{:S(2)}) async-start(), calls=%async_computation.5 | async-start | bytes 49152 | tf_op jit(solution)/shard_map/reduce_scatter | solution.py:62
  48.9 74.3 %reduce-scatter.5.cloned.1.call-start = ((), (), s32[]{:S(2)}) async-start(), calls=%async_computation.4 | async-start | bytes 294912 | tf_op jit(solution)/shard_map/reduce_scatter | solution.py:19
  50.8 6.3 %copy-start.1 = (f32[16,512]{1,0:T(8,128)S(1)}, f32[16,512]{1,0:T(8,128)}, u32[]{:S(2)}) copy-start(f32[16,512]{1,0:T(8,128)} %param.9) | copy-start | bytes 98308
  56.9 210.6 %reduce-scatter.11.cloned.1.call-start = ((), (), s32[]{:S(2)}) async-start(), calls=%async_computation.7 | async-start | bytes 49152 | tf_op jit(solution)/shard_map/reduce_scatter | solution.py:62
  261.6 70.4 %reduce-scatter.9.cloned.1.call-start = ((), (), s32[]{:S(2)}) async-start(), calls=%async_computation.6 | async-start | bytes 294912 | tf_op jit(solution)/shard_map/reduce_scatter | solution.py:19
Sparse Core Ops, SparseCore 0:
  49.1 8.3 reduce-scatter.6
  60.8 62.4 reduce-scatter.4
  261.7 4.6 reduce-scatter.10
  269.6 62.3 reduce-scatter.8
where the time goes:
time: 377 us
  blocking collectives  184 us (49%)
  waiting for transfers between devices  131 us (35%)
  other arithmetic  22.4 us (6%)
  matrix products  19.8 us (5%)
  between operations  14 us (4%)
  local copies, waits for them, and re-layouts  5.28 us (1%)
    reduce_scatter x2, waiting for transfers between devices, row_total(): return lax.psum_scatter(slab_sums, 'row', scatter_dimension=1, tiled=True)  130 us
    all_gather x2, blocking collectives, local(): slab_flat = lax.all_gather(rounded, 'row', axis=1, tiled=True)  62.9 us
    psum x1, blocking collectives, local(): squares = lax.psum(gram_matrix(residual, residual), ('row', 'col'))  57.7 us
    psum x1, blocking collectives, local(): curvature = lax.psum(gram_matrix(direction, mapped), ('row', 'col'))  30.2 us
    psum x1, blocking collectives, local(): renewed = lax.psum(gram_matrix(residual, residual), ('row', 'col'))  30 us
  transfers between devices with their start and end apart: 4, of which 3 were waited for; matrix products, arithmetic and copies ran while one was open for 3% of the time, Pallas kernels for 0%

commit v1 on v0

v1 whole, which is shorter than its diff:
```python
import functools

import jax
import jax.numpy as jnp
from jax import lax
from jax.experimental import pallas as pl
from jax.experimental.pallas import tpu as pltpu
from jax.sharding import PartitionSpec as P

MESH = pl.DeviceIdType.MESH
F32 = jnp.float32
BF16 = jnp.bfloat16
HIGH = lax.Precision.HIGHEST
HI_BAND, HI_SLAB, LO_BAND, LO_SLAB, OUT_SLAB0, OUT_BAND0, GRAM0, MAP_BAND, MAP_SLAB, OUT_SLAB1, OUT_BAND1, GRAM1 = range(12)


def loop(count, body, unroll=1):
    while count % unroll:
        unroll -= 1

    def step(i, carry):
        for u in range(unroll):
            body(i * unroll + u)
        return carry

    if count == unroll:
        step(0, 0)
    else:
        lax.fori_loop(0, count // unroll, step, 0)


def dot(left, right, dims):
    return lax.dot_general(left, right, (dims, ((), ())), precision=HIGH, preferred_element_type=F32)


def fast_dot(left, right, dims):
    return lax.dot_general(left, right, (dims, ((), ())), preferred_element_type=F32)


MM = ((1,), (0,))
MT = ((1,), (1,))


def split(x):
    hi = x.astype(BF16)
    return hi, (x - hi.astype(F32)).astype(BF16)


def eliminate(pairs):
    size = pairs[0][0].shape[0]
    row = lax.broadcasted_iota(jnp.int32, (size, size), 0)
    for k in range(size):
        out = []
        for a, b in pairs:
            scale = 1.0 / a[k : k + 1, k : k + 1]
            ra = a[k : k + 1, :] * scale
            rb = b[k : k + 1, :] * scale
            col = a[:, k : k + 1]
            out.append((jnp.where(row == k, ra, a - col * ra), jnp.where(row == k, rb, b - col * rb)))
        pairs = out
    return [b for _, b in pairs]


def kernel(
    n, chunks, rows_s, cols_s, cnt_s, probes, tiles_hbm, diag, sol, res,
    tiles, inv_v, inv_s, band_hi, band_lo, slab_hi, slab_lo, to_cols, to_rows,
    out_slab, in_slab, out_band, in_band, gram, map_band, map_slab, dir_band, dir_slab, dir_own,
    tile_sem, inv_sem, send, recv,
):
    slots, edge, _ = tiles.shape
    per = diag.shape[0]
    count = probes.shape[0]
    slab_tiles = n * per
    band_tiles = 2 * per
    g, r, c = lax.axis_index("groups"), lax.axis_index("row"), lax.axis_index("col")
    total = 2 * n
    line = 2 * r + c
    partner = (g, r, 1 - c)
    eye = (
        lax.broadcasted_iota(jnp.int32, (count, count), 0) == lax.broadcasted_iota(jnp.int32, (count, count), 1)
    ).astype(F32)

    def start(family, src, dst, device):
        pltpu.make_async_remote_copy(
            src_ref=src, dst_ref=dst, send_sem=send.at[family], recv_sem=recv.at[family],
            device_id=device, device_id_type=MESH,
        ).start()

    def to_slab(family, src, dst):
        def body(k):
            start(family, src(k), dst.at[n - 2 - k], (g, lax.rem(r + 1 + k, n), c))

        loop(n - 1, body, 7)

    def to_all(family, dst):
        def body(k):
            other = lax.rem(line + 1 + k, total)
            start(family, dst.at[total - 1], dst.at[total - 2 - k], (g, other // 2, lax.rem(other, 2)))

        loop(total - 1, body, 15)

    def await_ref(sem, ref):
        pltpu.make_async_copy(ref, ref, sem).wait()

    part = slots // chunks
    fetches = [
        pltpu.make_async_copy(tiles_hbm.at[pl.ds(i * part, part)], tiles.at[pl.ds(i * part, part)], tile_sem.at[i])
        for i in range(chunks)
    ]
    for fetch in fetches:
        fetch.start()

    barrier = pltpu.get_barrier_semaphore()

    def greet(k):
        other = lax.rem(line + 1 + k, total)
        pl.semaphore_signal(barrier, inc=1, device_id=(g, other // 2, lax.rem(other, 2)), device_id_type=MESH)

    loop(total - 1, greet, 15)

    place_id = lax.broadcasted_iota(jnp.int32, inv_v.shape, 1)
    held = jnp.full(inv_v.shape, slots, jnp.int32)
    for q in range(slots):
        place = (rows_s[q] % band_tiles) * slab_tiles + cols_s[q] // band_tiles * per + cols_s[q] % per
        place = jnp.where(cnt_s[q] > 0, place, -1)
        held = jnp.where(place_id == place, q, held)
    inv_v[...] = held
    to_smem = pltpu.make_async_copy(inv_v, inv_s, inv_sem)
    to_smem.start()
    to_cols[slots] = jnp.zeros(to_cols.shape[1:], F32)
    to_rows[slots] = jnp.zeros(to_rows.shape[1:], F32)

    for t in range(per):
        hi, lo = split(probes[:, t * edge : (t + 1) * edge])
        band_hi[c * per + t] = hi
        band_lo[c * per + t] = lo
        slab_hi[n - 1, t] = hi
        slab_lo[n - 1, t] = lo
    pl.semaphore_wait(barrier, total - 1)

    half = pl.ds(c * per, per)
    start(HI_BAND, band_hi.at[half], band_hi.at[half], partner)
    to_slab(HI_SLAB, lambda k: slab_hi.at[n - 1], slab_hi)
    start(LO_BAND, band_lo.at[half], band_lo.at[half], partner)
    to_slab(LO_SLAB, lambda k: slab_lo.at[n - 1], slab_lo)
    to_smem.wait()

    lane = lax.broadcasted_iota(jnp.int32, (count, edge), 1)

    def column_products(first, last, band):
        def body(i):
            q = first + i
            v = band(rows_s[q] % band_tiles)
            v = jnp.where(lane < cnt_s[q], v.astype(F32), 0.0).astype(BF16)
            to_cols[q] = fast_dot(v, tiles[q], MM)

        loop(last - first, body, 8)

    def row_products(slab):
        def body(q):
            owner = cols_s[q] // band_tiles
            v = slab(lax.rem(owner + 2 * n - r - 1, n), cols_s[q] % per)
            to_rows[q] = jnp.where(lane < cnt_s[q], fast_dot(v, tiles[q], MT), 0.0)

        loop(slots, body, 8)

    def send_slab(it, family):
        def body(k):
            owner = lax.rem(r + 1 + k, n)
            for t in range(per):
                acc = to_cols[inv_s[0, owner * per + t]]
                for b in range(1, band_tiles):
                    acc = acc + to_cols[inv_s[0, b * slab_tiles + owner * per + t]]
                out_slab[it, k, t] = acc

        def body_send(k):
            body(k)
            start(family, out_slab.at[it, k], in_slab.at[it, n - 2 - k], (g, lax.rem(r + 1 + k, n), c))

        loop(n - 1, body_send, 7)
        body(n - 1)

    def send_band(it, family):
        for place, base in enumerate(((1 - c) * per, c * per)):
            for t in range(per):
                acc = to_rows[inv_s[0, (base + t) * slab_tiles]]
                if slab_tiles <= 64:
                    for j in range(1, slab_tiles):
                        acc = acc + to_rows[inv_s[0, (base + t) * slab_tiles + j]]
                else:
                    acc = lax.fori_loop(
                        1, slab_tiles, lambda j, a: a + to_rows[inv_s[0, (base + t) * slab_tiles + j]], acc
                    )
                out_band[it, place, t] = acc
            if place == 0:
                start(family, out_band.at[it, 0], in_band.at[it], partner)

    def own_product(it, own_hi, slab_family, band_family):
        parts = [fast_dot(own_hi(t), diag[t], MM) + out_band[it, 1, t] + out_slab[it, n - 1, t] for t in range(per)]
        await_ref(recv.at[band_family], in_band.at[it])
        await_ref(recv.at[slab_family], in_slab.at[it])
        out = []
        for t in range(per):
            acc = parts[t] + in_band[it, t]
            if n <= 16:
                for k in range(n - 1):
                    acc = acc + in_slab[it, k, t]
            else:
                acc = lax.fori_loop(0, n - 1, lambda k, a: a + in_slab[it, k, t], acc)
            out.append(acc)
        return out

    def gram_total(it):
        await_ref(recv.at[GRAM0 if it == 0 else GRAM1], gram.at[it, pl.ds(0, total - 1)])
        acc = gram[it, lax.rem(2 * total - line - 1, total)]
        if total <= 32:
            for j in range(1, total):
                acc = acc + gram[it, lax.rem(j + 2 * total - line - 1, total)]
        else:
            acc = lax.fori_loop(1, total, lambda j, a: a + gram[it, lax.rem(j + 2 * total - line - 1, total)], acc)
        return acc

    await_ref(recv.at[HI_BAND], band_hi.at[half])
    for i in range(chunks):
        fetches[i].wait()
        column_products(i * part, (i + 1) * part, lambda b: band_hi[b])
    send_slab(0, OUT_SLAB0)
    await_ref(recv.at[HI_SLAB], slab_hi.at[pl.ds(0, n - 1)])
    row_products(lambda s, t: slab_hi[s, t])
    send_band(0, OUT_BAND0)
    own = own_product(0, lambda t: slab_hi[n - 1, t], OUT_SLAB0, OUT_BAND0)
    probe_tiles = [probes[:, t * edge : (t + 1) * edge] for t in range(per)]
    both = [jnp.concatenate([probe_tiles[t], own[t]], axis=0) for t in range(per)]
    block = sum(dot(x, x, MT) for x in both)
    width = 2 * count
    group = 8
    for i in range(width // group):
        gram[0, total - 1, :, i * width : (i + 1) * width] = block[i * group : (i + 1) * group, :]
    to_all(GRAM0, gram.at[0])
    for t in range(per):
        map_band[c * per + t] = own[t]
        map_slab[n - 1, t] = own[t]
    start(MAP_BAND, map_band.at[half], map_band.at[half], partner)
    to_slab(MAP_SLAB, lambda k: map_slab.at[n - 1], map_slab)
    packed = gram_total(0)
    block = jnp.concatenate([packed[:, i * width : (i + 1) * width] for i in range(width // group)], axis=0)
    squares, cross = block[:count, :count], block[:count, count:]
    cross_t, mapped_sq = block[count:, :count], block[count:, count:]
    step0, squares_inv = eliminate([((cross + cross_t) * 0.5, squares), (squares, eye)])
    step0_t = step0.T
    renewed = squares - dot(cross, step0, MM) + dot(step0_t, dot(mapped_sq, step0, MM) - cross_t, MM)
    blend = dot(squares_inv, renewed, MM)
    coef = jnp.concatenate([blend.T, -step0_t], axis=1)

    def next_direction(p, m):
        return p + dot(coef, jnp.concatenate([p, m], axis=0), MM)

    for t in range(per):
        d = next_direction(probe_tiles[t], own[t])
        dir_own[t] = d
        hi, lo = split(d)
        both_parts = jnp.concatenate([hi, lo], axis=0)
        dir_band[c * per + t] = both_parts
        dir_slab[n - 1, t] = both_parts
    await_ref(recv.at[LO_BAND], band_lo.at[half])
    await_ref(recv.at[MAP_BAND], map_band.at[half])
    for t in range(per):
        b = (1 - c) * per + t
        d = next_direction(band_hi[b].astype(F32) + band_lo[b].astype(F32), map_band[b])
        dir_band[b] = jnp.concatenate(split(d), axis=0)
    column_products(0, slots, lambda b: dir_band[b, :count])
    send_slab(1, OUT_SLAB1)
    await_ref(recv.at[LO_SLAB], slab_lo.at[pl.ds(0, n - 1)])
    await_ref(recv.at[MAP_SLAB], map_slab.at[pl.ds(0, n - 1)])

    def slab_direction(k):
        for t in range(per):
            d = next_direction(slab_hi[k, t].astype(F32) + slab_lo[k, t].astype(F32), map_slab[k, t])
            dir_slab[k, t] = jnp.concatenate(split(d), axis=0)

    loop(n - 1, slab_direction, 7)
    row_products(lambda s, t: dir_slab[s, t, :count])
    send_band(1, OUT_BAND1)

    def pair(d, m):
        return fast_dot(d, jnp.concatenate(split(m), axis=0), MT)

    def slab_pair(k):
        return sum(pair(dir_slab[k, t], out_slab[1, k, t]) for t in range(per))

    cross = lax.fori_loop(0, n, lambda k, a: a + slab_pair(k), jnp.zeros((width, width), F32))
    for t in range(per):
        cross = cross + pair(dir_band[(1 - c) * per + t], out_band[1, 0, t])
        cross = cross + pair(
            dir_slab[n - 1, t], out_band[1, 1, t] + fast_dot(dir_slab[n - 1, t, :count], diag[t], MM)
        )
    cross = cross[:count] + cross[count:]
    cross = cross[:, :count] + cross[:, count:]
    for i in range(count // group):
        gram[1, total - 1, :, i * count : (i + 1) * count] = cross[i * group : (i + 1) * group, :]
    gram[1, total - 1, :, width:] = jnp.zeros((group, gram.shape[3] - width), F32)
    to_all(GRAM1, gram.at[1])
    packed = gram_total(1)
    cross = jnp.concatenate([packed[:, i * count : (i + 1) * count] for i in range(count // group)], axis=0)
    (step1,) = eliminate([((cross + cross.T) * 0.5, renewed)])
    step1_t = step1.T
    own1 = own_product(1, lambda t: dir_slab[n - 1, t, :count], OUT_SLAB1, OUT_BAND1)
    for t in range(per):
        lanes = slice(t * edge, (t + 1) * edge)
        sol[:, lanes] = dot(step0_t, probe_tiles[t], MM) + dot(step1_t, dir_own[t], MM)
        res[:, lanes] = probe_tiles[t] - dot(step0_t, own[t], MM) - dot(step1_t, own1[t], MM)

    for family, ref in (
        (HI_BAND, band_hi.at[half]),
        (HI_SLAB, slab_hi.at[pl.ds(0, n - 1)]),
        (LO_BAND, band_lo.at[half]),
        (LO_SLAB, slab_lo.at[pl.ds(0, n - 1)]),
        (OUT_SLAB0, in_slab.at[0]),
        (OUT_BAND0, in_band.at[0]),
        (GRAM0, gram.at[0, pl.ds(0, total - 1)]),
        (MAP_BAND, map_band.at[half]),
        (MAP_SLAB, map_slab.at[pl.ds(0, n - 1)]),
        (OUT_SLAB1, in_slab.at[1]),
        (OUT_BAND1, in_band.at[1]),
        (GRAM1, gram.at[1, pl.ds(0, total - 1)]),
    ):
        await_ref(send.at[family], ref)


def solution(mesh):
    n = mesh.shape["row"]
    spread = ("groups", "row", "col")

    def local(probes, tiles, tile_rows, tile_cols, counts, diag_tiles):
        count, length = probes.shape
        slots, edge, _ = tiles.shape
        per = diag_tiles.shape[0]
        places = max(128, 2 * per * per * n)
        chunks = 4
        vmem = pl.BlockSpec(memory_space=pltpu.VMEM)
        smem = pl.BlockSpec(memory_space=pltpu.SMEM)
        scratch = [
            pltpu.VMEM(tiles.shape, BF16),
            pltpu.VMEM((1, places), jnp.int32),
            pltpu.SMEM((1, places), jnp.int32),
            pltpu.VMEM((2 * per, count, edge), BF16),
            pltpu.VMEM((2 * per, count, edge), BF16),
            pltpu.VMEM((n, per, count, edge), BF16),
            pltpu.VMEM((n, per, count, edge), BF16),
            pltpu.VMEM((slots + 1, count, edge), F32),
            pltpu.VMEM((slots + 1, count, edge), F32),
            pltpu.VMEM((2, n, per, count, edge), F32),
            pltpu.VMEM((2, n - 1, per, count, edge), F32),
            pltpu.VMEM((2, 2, per, count, edge), F32),
            pltpu.VMEM((2, per, count, edge), F32),
            pltpu.VMEM((2, 2 * n, 8, 128), F32),
            pltpu.VMEM((2 * per, count, edge), F32),
            pltpu.VMEM((n, per, count, edge), F32),
            pltpu.VMEM((2 * per, 2 * count, edge), BF16),
            pltpu.VMEM((n, per, 2 * count, edge), BF16),
            pltpu.VMEM((per, count, edge), F32),
            pltpu.SemaphoreType.DMA((chunks,)),
            pltpu.SemaphoreType.DMA,
            pltpu.SemaphoreType.DMA((12,)),
            pltpu.SemaphoreType.DMA((12,)),
        ]
        return pl.pallas_call(
            functools.partial(kernel, n, chunks),
            out_shape=(jax.ShapeDtypeStruct(probes.shape, F32),) * 2,
            in_specs=[smem, smem, smem, vmem, pl.BlockSpec(memory_space=pl.ANY), vmem],
            out_specs=(vmem, vmem),
            scratch_shapes=scratch,
            compiler_params=pltpu.CompilerParams(
                collective_id=0, has_side_effects=True, vmem_limit_bytes=48 * 2**20
            ),
        )(tile_rows, tile_cols, counts, probes, tiles, diag_tiles)

    return jax.shard_map(
        local,
        mesh=mesh,
        in_specs=(P(None, spread), P(spread, None, None), P(spread), P(spread), P(spread), P(spread, None, None)),
        out_specs=(P(None, spread), P(None, spread)),
        check_vma=False,
    )
```

time: 377 us -> 48.1 us (0.13)
  blocking collectives: 184 us -> 0 us
  waiting for transfers between devices: 131 us -> 0 us
  Pallas kernels: 0 us -> 40.1 us
  other arithmetic: 22.4 us -> 0 us
  matrix products: 19.8 us -> 0 us
  between operations: 14 us -> 0.65 us
    reduce_scatter x4 -> x0, waiting for transfers between devices: 130 us -> none  [the longest x2 130 us: row_total(): return lax.psum_scatter(slab_sums, 'row', scatter_dimension=1, tiled=True)]
    psum x3 -> x0, blocking collectives: 118 us -> none  [the longest x1 57.7 us: local(): squares = lax.psum(gram_matrix(residual, residual), ('row', 'col'))]
    all_gather x4 -> x0, blocking collectives: 66.6 us -> none  [the longest x2 62.9 us: local(): slab_flat = lax.all_gather(rounded, 'row', axis=1, tiled=True)]
    pallas_call x0 -> x1, Pallas kernels: none -> 40.1 us  [local(): pl.pallas_call(functools.partial(kernel, n, chunks), out_shape=(jax.Shape...]
    dot_general x15 -> x0, matrix products: 18.8 us -> none  [the longest x2 6.76 us: local(): jnp.einsum('pgb,gab->pga', src_cols, tiles, preferred_element_type=jnp.fl...]
    another operation x15 -> x0, other arithmetic: 12 us -> none  [the longest x9 6.4 us: small_solve(): lower = jnp.linalg.cholesky(matrix)]
    scatter-add x4 -> x0, other arithmetic: 7.47 us -> none  [the longest x2 3.76 us: local(): band_part = jnp.zeros((probe_count, band_tiles, tile_size), jnp.float32)....]
    unnamed x4 -> x14, local copies, waits for them, and re-layouts: 0.01 us -> 7.08 us
  transfers between devices with their start and end apart: 4 -> 0, of which waited for: 3 -> 0; matrix products, arithmetic and copies ran while one was open for 3% -> 0% of each run, Pallas kernels for 0% -> 0%
where the time goes in v1:
time: 48.1 us; the launch traced here: 47.8 us
  Pallas kernels  40.1 us (83%)
  local copies, waits for them, and re-layouts  7.08 us (15%)
  between operations  0.65 us (1%)
    pallas_call x1, Pallas kernels, local(): pl.pallas_call(functools.partial(kernel, n, chunks), out_shape=(jax.Shape...  40.1 us
    unnamed x14, local copies, waits for them, and re-layouts  7.08 us

profile of v1, /device:TPU:0, one launch (start us, length us, event | category | flops | bytes accessed | tf_op | source)
XLA Modules:
  0.0 47.8 jit_solution(9277038944826762346)
XLA Ops:
  0.6 0.0 copy-start
  0.6 2.2 %copy-done = bf16[32,256,256]{2,1,0:T(8,128)(2,1)S(1)} copy-done((bf16[32,256,256]{2,1,0:T(8,128)(2,1)S(1)}, bf16[32,256,256]{2,1,0:T(8,128)(2,1)}, u32[]{:S(2)}) %copy-start) | copy-done | bytes 4194328
  2.8 0.0 copy-start.1
  2.8 0.9 %copy-done.1 = bf16[2,256,256]{2,1,0:T(8,128)(2,1)S(1)} copy-done((bf16[2,256,256]{2,1,0:T(8,128)(2,1)S(1)}, bf16[2,256,256]{2,1,0:T(8,128)(2,1)}, u32[]{:S(2)}) %copy-start.1) | copy-done | bytes 262168
  3.8 0.0 copy-start.2
  3.8 0.8 %copy-done.2 = f32[16,512]{1,0:T(8,128)S(1)} copy-done((f32[16,512]{1,0:T(8,128)S(1)}, f32[16,512]{1,0:T(8,128)}, u32[]{:S(2)}) %copy-start.2) | copy-done | bytes 32792
  4.5 0.0 copy-start.3
  4.5 0.7 %copy-done.3 = s32[32]{0:T(128)S(1)} copy-done((s32[32]{0:T(128)S(1)}, s32[32]{0:T(128)}, u32[]{:S(2)}) %copy-start.3) | copy-done | bytes 152
  5.2 0.0 copy-start.4
  5.2 0.7 %copy-done.4 = s32[32]{0:T(128)S(1)} copy-done((s32[32]{0:T(128)S(1)}, s32[32]{0:T(128)}, u32[]{:S(2)}) %copy-start.4) | copy-done | bytes 152
  5.8 0.0 copy-start.5
  5.8 0.7 %copy-done.5 = s32[32]{0:T(128)S(1)} copy-done((s32[32]{0:T(128)S(1)}, s32[32]{0:T(128)}, u32[]{:S(2)}) %copy-start.5) | copy-done | bytes 152
  6.5 40.1 %shard_map.77 = (f32[16,512]{1,0:T(8,128)S(1)}, f32[16,512]{1,0:T(8,128)S(1)}) custom-call(s32[32]{0:T(128)S(1)} %copy-done.3, s32[32]{0:T(128)S(1)} %copy-done.4, s32[32]{0:T(128)S(1)} %copy-done.5, f32[16,512]{1,0:T(8,128)S(1)} %copy-done.2, bf16[32,256,256]{2,1,0:T(8,128)(2,1)S(1)} %copy-done, bf16[2,256,256]{2,1,0:T(8,128)(2,1)S(1)} %copy-done.1), custom_call_target="tpu_custom_call" | custom-call | tf_op jit(solution)/shard_map/pallas_call | solution.py:367
  46.6 0.6 %copy.10 = f32[16,512]{1,0:T(8,128)} copy(f32[16,512]{1,0:T(8,128)S(1)} %get-tuple-element.4) | data formatting | bytes 65536
  47.2 0.6 %copy.11 = f32[16,512]{1,0:T(8,128)} copy(f32[16,512]{1,0:T(8,128)S(1)} %get-tuple-element.5) | data formatting | bytes 65536
Async XLA Ops:
  0.6 2.2 %copy-start = (bf16[32,256,256]{2,1,0:T(8,128)(2,1)S(1)}, bf16[32,256,256]{2,1,0:T(8,128)(2,1)}, u32[]{:S(2)}) copy-start(bf16[32,256,256]{2,1,0:T(8,128)(2,1)} %tiles_hbm.1) | copy-start | bytes 12582916
  2.8 0.9 %copy-start.1 = (bf16[2,256,256]{2,1,0:T(8,128)(2,1)S(1)}, bf16[2,256,256]{2,1,0:T(8,128)(2,1)}, u32[]{:S(2)}) copy-start(bf16[2,256,256]{2,1,0:T(8,128)(2,1)} %diag.1) | copy-start | bytes 786436
  3.8 0.8 %copy-start.2 = (f32[16,512]{1,0:T(8,128)S(1)}, f32[16,512]{1,0:T(8,128)}, u32[]{:S(2)}) copy-start(f32[16,512]{1,0:T(8,128)} %probes.1) | copy-start | bytes 98308
  4.5 0.7 %copy-start.3 = (s32[32]{0:T(128)S(1)}, s32[32]{0:T(128)}, u32[]{:S(2)}) copy-start(s32[32]{0:T(128)} %rows_s.1) | copy-start | bytes 388
  5.2 0.7 %copy-start.4 = (s32[32]{0:T(128)S(1)}, s32[32]{0:T(128)}, u32[]{:S(2)}) copy-start(s32[32]{0:T(128)} %cols_s.1) | copy-start | bytes 388
  5.8 0.7 %copy-start.5 = (s32[32]{0:T(128)S(1)}, s32[32]{0:T(128)}, u32[]{:S(2)}) copy-start(s32[32]{0:T(128)} %cnt_s.1) | copy-start | bytes 388

commit v2 on v1

--- a/solution.py
+++ b/solution.py
@@ -62,10 +62,10 @@
 
 
 def kernel(
-    n, chunks, rows_s, cols_s, cnt_s, probes, tiles_hbm, diag, sol, res,
-    tiles, inv_v, inv_s, band_hi, band_lo, slab_hi, slab_lo, to_cols, to_rows,
-    out_slab, in_slab, out_band, in_band, gram, map_band, map_slab, dir_band, dir_slab, dir_own,
-    tile_sem, inv_sem, send, recv,
+    n, chunks, probes_hbm, tiles_hbm, rows_hbm, cols_hbm, cnt_hbm, diag_hbm, sol_hbm, res_hbm,
+    rows_s, cols_s, cnt_s, probes, diag, sol, res, tiles, inv_v, inv_s, band_hi, band_lo, slab_hi, slab_lo, to_cols, to_rows,
+    out_slab, cast_slab, in_slab, out_band, in_band, gram, map_band, map_slab, dir_band, dir_slab, dir_own,
+    tile_sem, small_sem, inv_sem, send, recv,
 ):
     slots, edge, _ = tiles.shape
     per = diag.shape[0]
@@ -102,6 +102,14 @@
     def await_ref(sem, ref):
         pltpu.make_async_copy(ref, ref, sem).wait()
 
+    small = [
+        pltpu.make_async_copy(src, dst, small_sem.at[i])
+        for i, (src, dst) in enumerate(
+            ((rows_hbm, rows_s), (cols_hbm, cols_s), (cnt_hbm, cnt_s), (probes_hbm, probes), (diag_hbm, diag))
+        )
+    ]
+    for fetch in small:
+        fetch.start()
     part = slots // chunks
     fetches = [
         pltpu.make_async_copy(tiles_hbm.at[pl.ds(i * part, part)], tiles.at[pl.ds(i * part, part)], tile_sem.at[i])
@@ -117,6 +125,9 @@
         pl.semaphore_signal(barrier, inc=1, device_id=(g, other // 2, lax.rem(other, 2)), device_id_type=MESH)
 
     loop(total - 1, greet, 15)
+
+    for fetch in small[:3]:
+        fetch.wait()
 
     place_id = lax.broadcasted_iota(jnp.int32, inv_v.shape, 1)
     held = jnp.full(inv_v.shape, slots, jnp.int32)
@@ -130,6 +141,7 @@
     to_cols[slots] = jnp.zeros(to_cols.shape[1:], F32)
     to_rows[slots] = jnp.zeros(to_rows.shape[1:], F32)
 
+    small[3].wait()
     for t in range(per):
         hi, lo = split(probes[:, t * edge : (t + 1) * edge])
         band_hi[c * per + t] = hi
@@ -175,7 +187,9 @@
 
         def body_send(k):
             body(k)
-            start(family, out_slab.at[it, k], in_slab.at[it, n - 2 - k], (g, lax.rem(r + 1 + k, n), c))
+            for t in range(per):
+                cast_slab[it, k, t] = out_slab[it, k, t].astype(BF16)
+            start(family, cast_slab.at[it, k], in_slab.at[it, n - 2 - k], (g, lax.rem(r + 1 + k, n), c))
 
         loop(n - 1, body_send, 7)
         body(n - 1)
@@ -204,9 +218,9 @@
             acc = parts[t] + in_band[it, t]
             if n <= 16:
                 for k in range(n - 1):
-                    acc = acc + in_slab[it, k, t]
+                    acc = acc + in_slab[it, k, t].astype(F32)
             else:
-                acc = lax.fori_loop(0, n - 1, lambda k, a: a + in_slab[it, k, t], acc)
+                acc = lax.fori_loop(0, n - 1, lambda k, a: a + in_slab[it, k, t].astype(F32), acc)
             out.append(acc)
         return out
 
@@ -228,6 +242,7 @@
     await_ref(recv.at[HI_SLAB], slab_hi.at[pl.ds(0, n - 1)])
     row_products(lambda s, t: slab_hi[s, t])
     send_band(0, OUT_BAND0)
+    small[4].wait()
     own = own_product(0, lambda t: slab_hi[n - 1, t], OUT_SLAB0, OUT_BAND0)
     probe_tiles = [probes[:, t * edge : (t + 1) * edge] for t in range(per)]
     both = [jnp.concatenate([probe_tiles[t], own[t]], axis=0) for t in range(per)]
@@ -310,6 +325,13 @@
         sol[:, lanes] = dot(step0_t, probe_tiles[t], MM) + dot(step1_t, dir_own[t], MM)
         res[:, lanes] = probe_tiles[t] - dot(step0_t, own[t], MM) - dot(step1_t, own1[t], MM)
 
+    out = [
+        pltpu.make_async_copy(src, dst, small_sem.at[i])
+        for i, (src, dst) in enumerate(((sol, sol_hbm), (res, res_hbm)))
+    ]
+    for copy in out:
+        copy.start()
+
     for family, ref in (
         (HI_BAND, band_hi.at[half]),
         (HI_SLAB, slab_hi.at[pl.ds(0, n - 1)]),
@@ -325,6 +347,8 @@
         (GRAM1, gram.at[1, pl.ds(0, total - 1)]),
     ):
         await_ref(send.at[family], ref)
+    for copy in out:
+        copy.wait()
 
 
 def solution(mesh):
@@ -337,9 +361,15 @@
         per = diag_tiles.shape[0]
         places = max(128, 2 * per * per * n)
         chunks = 4
-        vmem = pl.BlockSpec(memory_space=pltpu.VMEM)
-        smem = pl.BlockSpec(memory_space=pltpu.SMEM)
+        hbm = pl.BlockSpec(memory_space=pltpu.HBM)
         scratch = [
+            pltpu.SMEM((slots,), jnp.int32),
+            pltpu.SMEM((slots,), jnp.int32),
+            pltpu.SMEM((slots,), jnp.int32),
+            pltpu.VMEM(probes.shape, F32),
+            pltpu.VMEM(diag_tiles.shape, BF16),
+            pltpu.VMEM(probes.shape, F32),
+            pltpu.VMEM(probes.shape, F32),
             pltpu.VMEM(tiles.shape, BF16),
             pltpu.VMEM((1, places), jnp.int32),
             pltpu.SMEM((1, places), jnp.int32),
@@ -350,7 +380,8 @@
             pltpu.VMEM((slots + 1, count, edge), F32),
             pltpu.VMEM((slots + 1, count, edge), F32),
             pltpu.VMEM((2, n, per, count, edge), F32),
-            pltpu.VMEM((2, n - 1, per, count, edge), F32),
+            pltpu.VMEM((2, n - 1, per, count, edge), BF16),
+            pltpu.VMEM((2, n - 1, per, count, edge), BF16),
             pltpu.VMEM((2, 2, per, count, edge), F32),
             pltpu.VMEM((2, per, count, edge), F32),
             pltpu.VMEM((2, 2 * n, 8, 128), F32),
@@ -360,6 +391,7 @@
             pltpu.VMEM((n, per, 2 * count, edge), BF16),
             pltpu.VMEM((per, count, edge), F32),
             pltpu.SemaphoreType.DMA((chunks,)),
+            pltpu.SemaphoreType.DMA((5,)),
             pltpu.SemaphoreType.DMA,
             pltpu.SemaphoreType.DMA((12,)),
             pltpu.SemaphoreType.DMA((12,)),
@@ -367,13 +399,13 @@
         return pl.pallas_call(
             functools.partial(kernel, n, chunks),
             out_shape=(jax.ShapeDtypeStruct(probes.shape, F32),) * 2,
-            in_specs=[smem, smem, smem, vmem, pl.BlockSpec(memory_space=pl.ANY), vmem],
-            out_specs=(vmem, vmem),
+            in_specs=[hbm] * 6,
+            out_specs=(hbm, hbm),
             scratch_shapes=scratch,
             compiler_params=pltpu.CompilerParams(
-                collective_id=0, has_side_effects=True, vmem_limit_bytes=48 * 2**20
+                collective_id=0, has_side_effects=True, vmem_limit_bytes=56 * 2**20
             ),
-        )(tile_rows, tile_cols, counts, probes, tiles, diag_tiles)
+        )(probes, tiles, tile_rows, tile_cols, counts, diag_tiles)
 
     return jax.shard_map(
         local,

time: 48.1 us -> 39.8 us (0.83)
  local copies, waits for them, and re-layouts: 7.08 us -> 2.75 us
  Pallas kernels: 40.1 us -> 36.1 us
    unnamed x14 -> x2, local copies, waits for them, and re-layouts: 7.08 us -> 2.75 us
    pallas_call x1, Pallas kernels: 40.1 us -> 36.1 us  [local(): pl.pallas_call(functools.partial(kernel, n, chunks), out_shape=(jax.Shape...]
where the time goes in v2:
time: 39.8 us; the launch traced here: 39.5 us
  Pallas kernels  36.1 us (91%)
  local copies, waits for them, and re-layouts  2.75 us (7%)
  between operations  0.64 us (2%)
    pallas_call x1, Pallas kernels, local(): pl.pallas_call(functools.partial(kernel, n, chunks), out_shape=(jax.Shape...  36.1 us
    unnamed x2, local copies, waits for them, and re-layouts  2.75 us

profile of v2, /device:TPU:0, one launch (start us, length us, event | category | flops | bytes accessed | tf_op | source)
XLA Modules:
  0.0 39.5 jit_solution(787719440136410417)
XLA Ops:
  0.6 36.1 %shard_map.77 = (f32[16,512]{1,0:T(8,128)}, f32[16,512]{1,0:T(8,128)}) custom-call(f32[16,512]{1,0:T(8,128)} %probes_hbm.1, bf16[32,256,256]{2,1,0:T(8,128)(2,1)} %tiles_hbm.1, s32[32]{0:T(128)} %rows_hbm.1, s32[32]{0:T(128)} %cols_hbm.1, s32[32]{0:T(128)} %cnt_hbm.1, bf16[2,256,256]{2,1,0:T(8,128)(2,1)} %diag_hbm.1), custom_call_target="tpu_custom_call" | custom-call | tf_op jit(solution)/shard_map/pallas_call | solution.py:399
  36.8 1.4 %copy.10 = f32[16,512]{1,0:T(8,128)} copy(f32[16,512]{1,0:T(8,128)} %get-tuple-element.4) | data formatting | bytes 65536
  38.1 1.4 %copy.11 = f32[16,512]{1,0:T(8,128)} copy(f32[16,512]{1,0:T(8,128)} %get-tuple-element.5) | data formatting | bytes 65536

commit v3 on v2

--- a/solution.py
+++ b/solution.py
@@ -11,7 +11,7 @@
 F32 = jnp.float32
 BF16 = jnp.bfloat16
 HIGH = lax.Precision.HIGHEST
-HI_BAND, HI_SLAB, LO_BAND, LO_SLAB, OUT_SLAB0, OUT_BAND0, GRAM0, MAP_BAND, MAP_SLAB, OUT_SLAB1, OUT_BAND1, GRAM1 = range(12)
+HI_BAND, HI_SLAB, LO_BAND, LO_SLAB, OUT_SLAB0, OUT_BAND0, GRAM0, MAP_BAND, MAP_SLAB, OUT_SLAB1, OUT_BAND1, GRAM1, PAIR0, PAIR1 = range(14)
 
 
 def loop(count, body, unroll=1):
@@ -64,7 +64,7 @@
 def kernel(
     n, chunks, probes_hbm, tiles_hbm, rows_hbm, cols_hbm, cnt_hbm, diag_hbm, sol_hbm, res_hbm,
     rows_s, cols_s, cnt_s, probes, diag, sol, res, tiles, inv_v, inv_s, band_hi, band_lo, slab_hi, slab_lo, to_cols, to_rows,
-    out_slab, cast_slab, in_slab, out_band, in_band, gram, map_band, map_slab, dir_band, dir_slab, dir_own,
+    out_slab, cast_slab, in_slab, out_band, in_band, gram, pair_block, map_band, map_slab, dir_band, dir_slab, dir_own,
     tile_sem, small_sem, inv_sem, send, recv,
 ):
     slots, edge, _ = tiles.shape
@@ -73,8 +73,7 @@
     slab_tiles = n * per
     band_tiles = 2 * per
     g, r, c = lax.axis_index("groups"), lax.axis_index("row"), lax.axis_index("col")
-    total = 2 * n
-    line = 2 * r + c
+    group = 8
     partner = (g, r, 1 - c)
     eye = (
         lax.broadcasted_iota(jnp.int32, (count, count), 0) == lax.broadcasted_iota(jnp.int32, (count, count), 1)
@@ -91,13 +90,6 @@
             start(family, src(k), dst.at[n - 2 - k], (g, lax.rem(r + 1 + k, n), c))
 
         loop(n - 1, body, 7)
-
-    def to_all(family, dst):
-        def body(k):
-            other = lax.rem(line + 1 + k, total)
-            start(family, dst.at[total - 1], dst.at[total - 2 - k], (g, other // 2, lax.rem(other, 2)))
-
-        loop(total - 1, body, 15)
 
     def await_ref(sem, ref):
         pltpu.make_async_copy(ref, ref, sem).wait()
@@ -121,10 +113,10 @@
     barrier = pltpu.get_barrier_semaphore()
 
     def greet(k):
-        other = lax.rem(line + 1 + k, total)
-        pl.semaphore_signal(barrier, inc=1, device_id=(g, other // 2, lax.rem(other, 2)), device_id_type=MESH)
-
-    loop(total - 1, greet, 15)
+        pl.semaphore_signal(barrier, inc=1, device_id=(g, lax.rem(r + 1 + k, n), c), device_id_type=MESH)
+
+    pl.semaphore_signal(barrier, inc=1, device_id=partner, device_id_type=MESH)
+    loop(n - 1, greet, 7)
 
     for fetch in small[:3]:
         fetch.wait()
@@ -148,7 +140,7 @@
         band_lo[c * per + t] = lo
         slab_hi[n - 1, t] = hi
         slab_lo[n - 1, t] = lo
-    pl.semaphore_wait(barrier, total - 1)
+    pl.semaphore_wait(barrier, n)
 
     half = pl.ds(c * per, per)
     start(HI_BAND, band_hi.at[half], band_hi.at[half], partner)
@@ -224,15 +216,27 @@
             out.append(acc)
         return out
 
-    def gram_total(it):
-        await_ref(recv.at[GRAM0 if it == 0 else GRAM1], gram.at[it, pl.ds(0, total - 1)])
-        acc = gram[it, lax.rem(2 * total - line - 1, total)]
-        if total <= 32:
-            for j in range(1, total):
-                acc = acc + gram[it, lax.rem(j + 2 * total - line - 1, total)]
+    def gram_total(it, block, then=None):
+        columns = block.shape[1]
+        pair_block[it, 0] = jnp.zeros(pair_block.shape[2:], F32)
+        for i in range(block.shape[0] // group):
+            pair_block[it, 0, :, i * columns : (i + 1) * columns] = block[i * group : (i + 1) * group, :]
+        start(PAIR1 if it else PAIR0, pair_block.at[it, 0], pair_block.at[it, 1], partner)
+        await_ref(recv.at[PAIR1 if it else PAIR0], pair_block.at[it, 1])
+        gram[it, n - 1] = pair_block[it, 0] + pair_block[it, 1]
+        to_slab(GRAM1 if it else GRAM0, lambda k: gram.at[it, n - 1], gram.at[it])
+        if then is not None:
+            then()
+        await_ref(recv.at[GRAM1 if it else GRAM0], gram.at[it, pl.ds(0, n - 1)])
+        acc = gram[it, lax.rem(2 * n - r - 1, n)]
+        if n <= 16:
+            for j in range(1, n):
+                acc = acc + gram[it, lax.rem(j + 2 * n - r - 1, n)]
         else:
-            acc = lax.fori_loop(1, total, lambda j, a: a + gram[it, lax.rem(j + 2 * total - line - 1, total)], acc)
-        return acc
+            acc = lax.fori_loop(1, n, lambda j, a: a + gram[it, lax.rem(j + 2 * n - r - 1, n)], acc)
+        return jnp.concatenate(
+            [acc[:, i * columns : (i + 1) * columns] for i in range(block.shape[0] // group)], axis=0
+        )
 
     await_ref(recv.at[HI_BAND], band_hi.at[half])
     for i in range(chunks):
@@ -248,17 +252,14 @@
     both = [jnp.concatenate([probe_tiles[t], own[t]], axis=0) for t in range(per)]
     block = sum(dot(x, x, MT) for x in both)
     width = 2 * count
-    group = 8
-    for i in range(width // group):
-        gram[0, total - 1, :, i * width : (i + 1) * width] = block[i * group : (i + 1) * group, :]
-    to_all(GRAM0, gram.at[0])
     for t in range(per):
         map_band[c * per + t] = own[t]
         map_slab[n - 1, t] = own[t]
-    start(MAP_BAND, map_band.at[half], map_band.at[half], partner)
-    to_slab(MAP_SLAB, lambda k: map_slab.at[n - 1], map_slab)
-    packed = gram_total(0)
-    block = jnp.concatenate([packed[:, i * width : (i + 1) * width] for i in range(width // group)], axis=0)
+    def send_mapped():
+        start(MAP_BAND, map_band.at[half], map_band.at[half], partner)
+        to_slab(MAP_SLAB, lambda k: map_slab.at[n - 1], map_slab)
+
+    block = gram_total(0, block, send_mapped)
     squares, cross = block[:count, :count], block[:count, count:]
     cross_t, mapped_sq = block[count:, :count], block[count:, count:]
     step0, squares_inv = eliminate([((cross + cross_t) * 0.5, squares), (squares, eye)])
@@ -311,12 +312,7 @@
         )
     cross = cross[:count] + cross[count:]
     cross = cross[:, :count] + cross[:, count:]
-    for i in range(count // group):
-        gram[1, total - 1, :, i * count : (i + 1) * count] = cross[i * group : (i + 1) * group, :]
-    gram[1, total - 1, :, width:] = jnp.zeros((group, gram.shape[3] - width), F32)
-    to_all(GRAM1, gram.at[1])
-    packed = gram_total(1)
-    cross = jnp.concatenate([packed[:, i * count : (i + 1) * count] for i in range(count // group)], axis=0)
+    cross = gram_total(1, cross)
     (step1,) = eliminate([((cross + cross.T) * 0.5, renewed)])
     step1_t = step1.T
     own1 = own_product(1, lambda t: dir_slab[n - 1, t, :count], OUT_SLAB1, OUT_BAND1)
@@ -339,12 +335,14 @@
         (LO_SLAB, slab_lo.at[pl.ds(0, n - 1)]),
         (OUT_SLAB0, in_slab.at[0]),
         (OUT_BAND0, in_band.at[0]),
-        (GRAM0, gram.at[0, pl.ds(0, total - 1)]),
+        (GRAM0, gram.at[0, pl.ds(0, n - 1)]),
         (MAP_BAND, map_band.at[half]),
         (MAP_SLAB, map_slab.at[pl.ds(0, n - 1)]),
         (OUT_SLAB1, in_slab.at[1]),
         (OUT_BAND1, in_band.at[1]),
-        (GRAM1, gram.at[1, pl.ds(0, total - 1)]),
+        (GRAM1, gram.at[1, pl.ds(0, n - 1)]),
+        (PAIR0, pair_block.at[0, 1]),
+        (PAIR1, pair_block.at[1, 1]),
     ):
         await_ref(send.at[family], ref)
     for copy in out:
@@ -384,7 +382,8 @@
             pltpu.VMEM((2, n - 1, per, count, edge), BF16),
             pltpu.VMEM((2, 2, per, count, edge), F32),
             pltpu.VMEM((2, per, count, edge), F32),
-            pltpu.VMEM((2, 2 * n, 8, 128), F32),
+            pltpu.VMEM((2, n, 8, 128), F32),
+            pltpu.VMEM((2, 2, 8, 128), F32),
             pltpu.VMEM((2 * per, count, edge), F32),
             pltpu.VMEM((n, per, count, edge), F32),
             pltpu.VMEM((2 * per, 2 * count, edge), BF16),
@@ -393,8 +392,8 @@
             pltpu.SemaphoreType.DMA((chunks,)),
             pltpu.SemaphoreType.DMA((5,)),
             pltpu.SemaphoreType.DMA,
-            pltpu.SemaphoreType.DMA((12,)),
-            pltpu.SemaphoreType.DMA((12,)),
+            pltpu.SemaphoreType.DMA((14,)),
+            pltpu.SemaphoreType.DMA((14,)),
         ]
         return pl.pallas_call(
             functools.partial(kernel, n, chunks),

time: 39.8 us -> 40.2 us (1.010)
  Pallas kernels: 36.1 us -> 36.6 us
    pallas_call x1, Pallas kernels: 36.1 us -> 36.6 us  [local(): pl.pallas_call(functools.partial(kernel, n, chunks), out_shape=(jax.Shape...]
where the time goes in v3:
time: 40.2 us; the launch traced here: 40 us
  Pallas kernels  36.6 us (91%)
  local copies, waits for them, and re-layouts  2.75 us (7%)
  between operations  0.64 us (2%)
    pallas_call x1, Pallas kernels, local(): pl.pallas_call(functools.partial(kernel, n, chunks), out_shape=(jax.Shape...  36.6 us
    unnamed x2, local copies, waits for them, and re-layouts  2.75 us

profile of v3, /device:TPU:0, one launch (start us, length us, event | category | flops | bytes accessed | tf_op | source)
XLA Modules:
  0.0 40.0 jit_solution(11056635172331485436)
XLA Ops:
  0.6 36.6 %shard_map.77 = (f32[16,512]{1,0:T(8,128)}, f32[16,512]{1,0:T(8,128)}) custom-call(f32[16,512]{1,0:T(8,128)} %probes_hbm.1, bf16[32,256,256]{2,1,0:T(8,128)(2,1)} %tiles_hbm.1, s32[32]{0:T(128)} %rows_hbm.1, s32[32]{0:T(128)} %cols_hbm.1, s32[32]{0:T(128)} %cnt_hbm.1, bf16[2,256,256]{2,1,0:T(8,128)(2,1)} %diag_hbm.1), custom_call_target="tpu_custom_call" | custom-call | tf_op jit(solution)/shard_map/pallas_call | solution.py:398
  37.2 1.4 %copy.10 = f32[16,512]{1,0:T(8,128)} copy(f32[16,512]{1,0:T(8,128)} %get-tuple-element.4) | data formatting | bytes 65536
  38.6 1.4 %copy.11 = f32[16,512]{1,0:T(8,128)} copy(f32[16,512]{1,0:T(8,128)} %get-tuple-element.5) | data formatting | bytes 65536

commit v4 on v3

--- a/solution.py
+++ b/solution.py
@@ -11,7 +11,7 @@
 F32 = jnp.float32
 BF16 = jnp.bfloat16
 HIGH = lax.Precision.HIGHEST
-HI_BAND, HI_SLAB, LO_BAND, LO_SLAB, OUT_SLAB0, OUT_BAND0, GRAM0, MAP_BAND, MAP_SLAB, OUT_SLAB1, OUT_BAND1, GRAM1, PAIR0, PAIR1 = range(14)
+BAND0, SLAB0, OUT_SLAB0, OUT_BAND0, GRAM0, PAIR0, BAND1, SLAB1, OUT_SLAB1, OUT_BAND1, GRAM1, PAIR1 = range(12)
 
 
 def loop(count, body, unroll=1):
@@ -39,11 +39,6 @@
 
 MM = ((1,), (0,))
 MT = ((1,), (1,))
-
-
-def split(x):
-    hi = x.astype(BF16)
-    return hi, (x - hi.astype(F32)).astype(BF16)
 
 
 def eliminate(pairs):
@@ -63,8 +58,8 @@
 
 def kernel(
     n, chunks, probes_hbm, tiles_hbm, rows_hbm, cols_hbm, cnt_hbm, diag_hbm, sol_hbm, res_hbm,
-    rows_s, cols_s, cnt_s, probes, diag, sol, res, tiles, inv_v, inv_s, band_hi, band_lo, slab_hi, slab_lo, to_cols, to_rows,
-    out_slab, cast_slab, in_slab, out_band, in_band, gram, pair_block, map_band, map_slab, dir_band, dir_slab, dir_own,
+    rows_s, cols_s, cnt_s, probes, diag, sol, res, tiles, inv_v, inv_s, band, slab, to_cols, to_rows,
+    out_slab, cast_slab, in_slab, out_band, in_band, gram, pair_block,
     tile_sem, small_sem, inv_sem, send, recv,
 ):
     slots, edge, _ = tiles.shape
@@ -134,36 +129,41 @@
     to_rows[slots] = jnp.zeros(to_rows.shape[1:], F32)
 
     small[3].wait()
-    for t in range(per):
-        hi, lo = split(probes[:, t * edge : (t + 1) * edge])
-        band_hi[c * per + t] = hi
-        band_lo[c * per + t] = lo
-        slab_hi[n - 1, t] = hi
-        slab_lo[n - 1, t] = lo
+    probe_tiles = [probes[:, t * edge : (t + 1) * edge] for t in range(per)]
+
+    def place_own(it, direction):
+        for t in range(per):
+            rounded = direction[t].astype(BF16)
+            band[it, c * per + t] = rounded
+            slab[it, n - 1, t] = rounded
+
+    place_own(0, probe_tiles)
     pl.semaphore_wait(barrier, n)
 
     half = pl.ds(c * per, per)
-    start(HI_BAND, band_hi.at[half], band_hi.at[half], partner)
-    to_slab(HI_SLAB, lambda k: slab_hi.at[n - 1], slab_hi)
-    start(LO_BAND, band_lo.at[half], band_lo.at[half], partner)
-    to_slab(LO_SLAB, lambda k: slab_lo.at[n - 1], slab_lo)
+
+    def gather(it, band_family, slab_family):
+        start(band_family, band.at[it, half], band.at[it, half], partner)
+        to_slab(slab_family, lambda k: slab.at[it, n - 1], slab.at[it])
+
+    gather(0, BAND0, SLAB0)
     to_smem.wait()
 
     lane = lax.broadcasted_iota(jnp.int32, (count, edge), 1)
 
-    def column_products(first, last, band):
+    def column_products(it, first, last):
         def body(i):
             q = first + i
-            v = band(rows_s[q] % band_tiles)
+            v = band[it, rows_s[q] % band_tiles]
             v = jnp.where(lane < cnt_s[q], v.astype(F32), 0.0).astype(BF16)
             to_cols[q] = fast_dot(v, tiles[q], MM)
 
         loop(last - first, body, 8)
 
-    def row_products(slab):
+    def row_products(it):
         def body(q):
             owner = cols_s[q] // band_tiles
-            v = slab(lax.rem(owner + 2 * n - r - 1, n), cols_s[q] % per)
+            v = slab[it, lax.rem(owner + 2 * n - r - 1, n), cols_s[q] % per]
             to_rows[q] = jnp.where(lane < cnt_s[q], fast_dot(v, tiles[q], MT), 0.0)
 
         loop(slots, body, 8)
@@ -201,8 +201,8 @@
             if place == 0:
                 start(family, out_band.at[it, 0], in_band.at[it], partner)
 
-    def own_product(it, own_hi, slab_family, band_family):
-        parts = [fast_dot(own_hi(t), diag[t], MM) + out_band[it, 1, t] + out_slab[it, n - 1, t] for t in range(per)]
+    def own_product(it, slab_family, band_family):
+        parts = [fast_dot(slab[it, n - 1, t], diag[t], MM) + out_band[it, 1, t] + out_slab[it, n - 1, t] for t in range(per)]
         await_ref(recv.at[band_family], in_band.at[it])
         await_ref(recv.at[slab_family], in_slab.at[it])
         out = []
@@ -216,7 +216,7 @@
             out.append(acc)
         return out
 
-    def gram_total(it, block, then=None):
+    def gram_total(it, block):
         columns = block.shape[1]
         pair_block[it, 0] = jnp.zeros(pair_block.shape[2:], F32)
         for i in range(block.shape[0] // group):
@@ -225,8 +225,6 @@
         await_ref(recv.at[PAIR1 if it else PAIR0], pair_block.at[it, 1])
         gram[it, n - 1] = pair_block[it, 0] + pair_block[it, 1]
         to_slab(GRAM1 if it else GRAM0, lambda k: gram.at[it, n - 1], gram.at[it])
-        if then is not None:
-            then()
         await_ref(recv.at[GRAM1 if it else GRAM0], gram.at[it, pl.ds(0, n - 1)])
         acc = gram[it, lax.rem(2 * n - r - 1, n)]
         if n <= 16:
@@ -238,28 +236,19 @@
             [acc[:, i * columns : (i + 1) * columns] for i in range(block.shape[0] // group)], axis=0
         )
 
-    await_ref(recv.at[HI_BAND], band_hi.at[half])
+    await_ref(recv.at[BAND0], band.at[0, half])
     for i in range(chunks):
         fetches[i].wait()
-        column_products(i * part, (i + 1) * part, lambda b: band_hi[b])
+        column_products(0, i * part, (i + 1) * part)
     send_slab(0, OUT_SLAB0)
-    await_ref(recv.at[HI_SLAB], slab_hi.at[pl.ds(0, n - 1)])
-    row_products(lambda s, t: slab_hi[s, t])
+    await_ref(recv.at[SLAB0], slab.at[0, pl.ds(0, n - 1)])
+    row_products(0)
     send_band(0, OUT_BAND0)
     small[4].wait()
-    own = own_product(0, lambda t: slab_hi[n - 1, t], OUT_SLAB0, OUT_BAND0)
-    probe_tiles = [probes[:, t * edge : (t + 1) * edge] for t in range(per)]
+    own = own_product(0, OUT_SLAB0, OUT_BAND0)
     both = [jnp.concatenate([probe_tiles[t], own[t]], axis=0) for t in range(per)]
     block = sum(dot(x, x, MT) for x in both)
-    width = 2 * count
-    for t in range(per):
-        map_band[c * per + t] = own[t]
-        map_slab[n - 1, t] = own[t]
-    def send_mapped():
-        start(MAP_BAND, map_band.at[half], map_band.at[half], partner)
-        to_slab(MAP_SLAB, lambda k: map_slab.at[n - 1], map_slab)
-
-    block = gram_total(0, block, send_mapped)
+    block = gram_total(0, block)
     squares, cross = block[:count, :count], block[:count, count:]
     cross_t, mapped_sq = block[count:, :count], block[count:, count:]
     step0, squares_inv = eliminate([((cross + cross_t) * 0.5, squares), (squares, eye)])
@@ -268,57 +257,22 @@
     blend = dot(squares_inv, renewed, MM)
     coef = jnp.concatenate([blend.T, -step0_t], axis=1)
 
-    def next_direction(p, m):
-        return p + dot(coef, jnp.concatenate([p, m], axis=0), MM)
-
-    for t in range(per):
-        d = next_direction(probe_tiles[t], own[t])
-        dir_own[t] = d
-        hi, lo = split(d)
-        both_parts = jnp.concatenate([hi, lo], axis=0)
-        dir_band[c * per + t] = both_parts
-        dir_slab[n - 1, t] = both_parts
-    await_ref(recv.at[LO_BAND], band_lo.at[half])
-    await_ref(recv.at[MAP_BAND], map_band.at[half])
-    for t in range(per):
-        b = (1 - c) * per + t
-        d = next_direction(band_hi[b].astype(F32) + band_lo[b].astype(F32), map_band[b])
-        dir_band[b] = jnp.concatenate(split(d), axis=0)
-    column_products(0, slots, lambda b: dir_band[b, :count])
+    direction = [probe_tiles[t] + dot(coef, both[t], MM) for t in range(per)]
+    place_own(1, direction)
+    gather(1, BAND1, SLAB1)
+    await_ref(recv.at[BAND1], band.at[1, half])
+    column_products(1, 0, slots)
     send_slab(1, OUT_SLAB1)
-    await_ref(recv.at[LO_SLAB], slab_lo.at[pl.ds(0, n - 1)])
-    await_ref(recv.at[MAP_SLAB], map_slab.at[pl.ds(0, n - 1)])
-
-    def slab_direction(k):
-        for t in range(per):
-            d = next_direction(slab_hi[k, t].astype(F32) + slab_lo[k, t].astype(F32), map_slab[k, t])
-            dir_slab[k, t] = jnp.concatenate(split(d), axis=0)
-
-    loop(n - 1, slab_direction, 7)
-    row_products(lambda s, t: dir_slab[s, t, :count])
+    await_ref(recv.at[SLAB1], slab.at[1, pl.ds(0, n - 1)])
+    row_products(1)
     send_band(1, OUT_BAND1)
-
-    def pair(d, m):
-        return fast_dot(d, jnp.concatenate(split(m), axis=0), MT)
-
-    def slab_pair(k):
-        return sum(pair(dir_slab[k, t], out_slab[1, k, t]) for t in range(per))
-
-    cross = lax.fori_loop(0, n, lambda k, a: a + slab_pair(k), jnp.zeros((width, width), F32))
-    for t in range(per):
-        cross = cross + pair(dir_band[(1 - c) * per + t], out_band[1, 0, t])
-        cross = cross + pair(
-            dir_slab[n - 1, t], out_band[1, 1, t] + fast_dot(dir_slab[n - 1, t, :count], diag[t], MM)
-        )
-    cross = cross[:count] + cross[count:]
-    cross = cross[:, :count] + cross[:, count:]
-    cross = gram_total(1, cross)
+    own1 = own_product(1, OUT_SLAB1, OUT_BAND1)
+    cross = gram_total(1, sum(dot(direction[t], own1[t], MT) for t in range(per)))
     (step1,) = eliminate([((cross + cross.T) * 0.5, renewed)])
     step1_t = step1.T
-    own1 = own_product(1, lambda t: dir_slab[n - 1, t, :count], OUT_SLAB1, OUT_BAND1)
     for t in range(per):
         lanes = slice(t * edge, (t + 1) * edge)
-        sol[:, lanes] = dot(step0_t, probe_tiles[t], MM) + dot(step1_t, dir_own[t], MM)
+        sol[:, lanes] = dot(step0_t, probe_tiles[t], MM) + dot(step1_t, direction[t], MM)
         res[:, lanes] = probe_tiles[t] - dot(step0_t, own[t], MM) - dot(step1_t, own1[t], MM)
 
     out = [
@@ -329,19 +283,17 @@
         copy.start()
 
     for family, ref in (
-        (HI_BAND, band_hi.at[half]),
-        (HI_SLAB, slab_hi.at[pl.ds(0, n - 1)]),
-        (LO_BAND, band_lo.at[half]),
-        (LO_SLAB, slab_lo.at[pl.ds(0, n - 1)]),
+        (BAND0, band.at[0, half]),
+        (SLAB0, slab.at[0, pl.ds(0, n - 1)]),
         (OUT_SLAB0, in_slab.at[0]),
         (OUT_BAND0, in_band.at[0]),
         (GRAM0, gram.at[0, pl.ds(0, n - 1)]),
-        (MAP_BAND, map_band.at[half]),
-        (MAP_SLAB, map_slab.at[pl.ds(0, n - 1)]),
+        (PAIR0, pair_block.at[0, 1]),
+        (BAND1, band.at[1, half]),
+        (SLAB1, slab.at[1, pl.ds(0, n - 1)]),
         (OUT_SLAB1, in_slab.at[1]),
         (OUT_BAND1, in_band.at[1]),
         (GRAM1, gram.at[1, pl.ds(0, n - 1)]),
-        (PAIR0, pair_block.at[0, 1]),
         (PAIR1, pair_block.at[1, 1]),
     ):
         await_ref(send.at[family], ref)
@@ -371,10 +323,8 @@
             pltpu.VMEM(tiles.shape, BF16),
             pltpu.VMEM((1, places), jnp.int32),
             pltpu.SMEM((1, places), jnp.int32),
-            pltpu.VMEM((2 * per, count, edge), BF16),
-            pltpu.VMEM((2 * per, count, edge), BF16),
-            pltpu.VMEM((n, per, count, edge), BF16),
-            pltpu.VMEM((n, per, count, edge), BF16),
+            pltpu.VMEM((2, 2 * per, count, edge), BF16),
+            pltpu.VMEM((2, n, per, count, edge), BF16),
             pltpu.VMEM((slots + 1, count, edge), F32),
             pltpu.VMEM((slots + 1, count, edge), F32),
             pltpu.VMEM((2, n, per, count, edge), F32),
@@ -384,16 +334,11 @@
             pltpu.VMEM((2, per, count, edge), F32),
             pltpu.VMEM((2, n, 8, 128), F32),
             pltpu.VMEM((2, 2, 8, 128), F32),
-            pltpu.VMEM((2 * per, count, edge), F32),
-            pltpu.VMEM((n, per, count, edge), F32),
-            pltpu.VMEM((2 * per, 2 * count, edge), BF16),
-            pltpu.VMEM((n, per, 2 * count, edge), BF16),
-            pltpu.VMEM((per, count, edge), F32),
             pltpu.SemaphoreType.DMA((chunks,)),
             pltpu.SemaphoreType.DMA((5,)),
             pltpu.SemaphoreType.DMA,
-            pltpu.SemaphoreType.DMA((14,)),
-            pltpu.SemaphoreType.DMA((14,)),
+            pltpu.SemaphoreType.DMA((12,)),
+            pltpu.SemaphoreType.DMA((12,)),
         ]
         return pl.pallas_call(
             functools.partial(kernel, n, chunks),

time: 40.2 us -> 40.9 us (1.017)
  Pallas kernels: 36.6 us -> 37.2 us
    pallas_call x1, Pallas kernels: 36.6 us -> 37.2 us  [local(): pl.pallas_call(functools.partial(kernel, n, chunks), out_shape=(jax.Shape...]
where the time goes in v4:
time: 40.9 us; the launch traced here: 40.6 us
  Pallas kernels  37.2 us (91%)
  local copies, waits for them, and re-layouts  2.75 us (7%)
  between operations  0.64 us (2%)
    pallas_call x1, Pallas kernels, local(): pl.pallas_call(functools.partial(kernel, n, chunks), out_shape=(jax.Shape...  37.2 us
    unnamed x2, local copies, waits for them, and re-layouts  2.75 us

profile of v4, /device:TPU:0, one launch (start us, length us, event | category | flops | bytes accessed | tf_op | source)
XLA Modules:
  0.0 40.6 jit_solution(9120891353367945961)
XLA Ops:
  0.6 37.2 %shard_map.77 = (f32[16,512]{1,0:T(8,128)}, f32[16,512]{1,0:T(8,128)}) custom-call(f32[16,512]{1,0:T(8,128)} %probes_hbm.1, bf16[32,256,256]{2,1,0:T(8,128)(2,1)} %tiles_hbm.1, s32[32]{0:T(128)} %rows_hbm.1, s32[32]{0:T(128)} %cols_hbm.1, s32[32]{0:T(128)} %cnt_hbm.1, bf16[2,256,256]{2,1,0:T(8,128)(2,1)} %diag_hbm.1), custom_call_target="tpu_custom_call" | custom-call | tf_op jit(solution)/shard_map/pallas_call | solution.py:343
  37.9 1.4 %copy.10 = f32[16,512]{1,0:T(8,128)} copy(f32[16,512]{1,0:T(8,128)} %get-tuple-element.4) | data formatting | bytes 65536
  39.2 1.4 %copy.11 = f32[16,512]{1,0:T(8,128)} copy(f32[16,512]{1,0:T(8,128)} %get-tuple-element.5) | data formatting | bytes 65536

commit v5 on v4

--- a/solution.py
+++ b/solution.py
@@ -11,7 +11,7 @@
 F32 = jnp.float32
 BF16 = jnp.bfloat16
 HIGH = lax.Precision.HIGHEST
-BAND0, SLAB0, OUT_SLAB0, OUT_BAND0, GRAM0, PAIR0, BAND1, SLAB1, OUT_SLAB1, OUT_BAND1, GRAM1, PAIR1 = range(12)
+BAND0, SLAB0, OUT_SLAB0, OUT_BAND0, GRAM0, BAND1, SLAB1, OUT_SLAB1, OUT_BAND1, GRAM1 = range(10)
 
 
 def loop(count, body, unroll=1):
@@ -39,6 +39,23 @@
 
 MM = ((1,), (0,))
 MT = ((1,), (1,))
+
+
+def gram_block(lefts, rights):
+    rows = lefts[0].shape[0]
+
+    def thirds(x):
+        hi = x.astype(BF16)
+        rest = x - hi.astype(F32)
+        mid = rest.astype(BF16)
+        low = (rest - mid.astype(F32)).astype(BF16)
+        return jnp.concatenate([hi, mid, low], axis=0)
+
+    left = [thirds(x) for x in lefts]
+    right = left if rights is lefts else [thirds(x) for x in rights]
+    full = sum(fast_dot(a, b, MT) for a, b in zip(left, right))
+    full = full[2 * rows :] + full[rows : 2 * rows] + full[:rows]
+    return full[:, 2 * rows :] + full[:, rows : 2 * rows] + full[:, :rows]
 
 
 def eliminate(pairs):
@@ -59,7 +76,7 @@
 def kernel(
     n, chunks, probes_hbm, tiles_hbm, rows_hbm, cols_hbm, cnt_hbm, diag_hbm, sol_hbm, res_hbm,
     rows_s, cols_s, cnt_s, probes, diag, sol, res, tiles, inv_v, inv_s, band, slab, to_cols, to_rows,
-    out_slab, cast_slab, in_slab, out_band, in_band, gram, pair_block,
+    out_slab, cast_slab, in_slab, out_band, in_band, gram,
     tile_sem, small_sem, inv_sem, send, recv,
 ):
     slots, edge, _ = tiles.shape
@@ -68,6 +85,8 @@
     slab_tiles = n * per
     band_tiles = 2 * per
     g, r, c = lax.axis_index("groups"), lax.axis_index("row"), lax.axis_index("col")
+    total = 2 * n
+    line = 2 * r + c
     group = 8
     partner = (g, r, 1 - c)
     eye = (
@@ -108,10 +127,10 @@
     barrier = pltpu.get_barrier_semaphore()
 
     def greet(k):
-        pl.semaphore_signal(barrier, inc=1, device_id=(g, lax.rem(r + 1 + k, n), c), device_id_type=MESH)
-
-    pl.semaphore_signal(barrier, inc=1, device_id=partner, device_id_type=MESH)
-    loop(n - 1, greet, 7)
+        other = lax.rem(line + 1 + k, total)
+        pl.semaphore_signal(barrier, inc=1, device_id=(g, other // 2, lax.rem(other, 2)), device_id_type=MESH)
+
+    loop(total - 1, greet, 15)
 
     for fetch in small[:3]:
         fetch.wait()
@@ -138,7 +157,7 @@
             slab[it, n - 1, t] = rounded
 
     place_own(0, probe_tiles)
-    pl.semaphore_wait(barrier, n)
+    pl.semaphore_wait(barrier, total - 1)
 
     half = pl.ds(c * per, per)
 
@@ -216,22 +235,26 @@
             out.append(acc)
         return out
 
-    def gram_total(it, block):
+    def gram_total(it, family, block):
         columns = block.shape[1]
-        pair_block[it, 0] = jnp.zeros(pair_block.shape[2:], F32)
+        gram[it, total - 1] = jnp.zeros(gram.shape[2:], F32)
         for i in range(block.shape[0] // group):
-            pair_block[it, 0, :, i * columns : (i + 1) * columns] = block[i * group : (i + 1) * group, :]
-        start(PAIR1 if it else PAIR0, pair_block.at[it, 0], pair_block.at[it, 1], partner)
-        await_ref(recv.at[PAIR1 if it else PAIR0], pair_block.at[it, 1])
-        gram[it, n - 1] = pair_block[it, 0] + pair_block[it, 1]
-        to_slab(GRAM1 if it else GRAM0, lambda k: gram.at[it, n - 1], gram.at[it])
-        await_ref(recv.at[GRAM1 if it else GRAM0], gram.at[it, pl.ds(0, n - 1)])
-        acc = gram[it, lax.rem(2 * n - r - 1, n)]
-        if n <= 16:
-            for j in range(1, n):
-                acc = acc + gram[it, lax.rem(j + 2 * n - r - 1, n)]
+            gram[it, total - 1, :, i * columns : (i + 1) * columns] = block[i * group : (i + 1) * group, :]
+
+        def body(k):
+            other = lax.rem(line + 1 + k, total)
+            start(
+                family, gram.at[it, total - 1], gram.at[it, total - 2 - k], (g, other // 2, lax.rem(other, 2))
+            )
+
+        loop(total - 1, body, 15)
+        await_ref(recv.at[family], gram.at[it, pl.ds(0, total - 1)])
+        acc = gram[it, lax.rem(2 * total - line - 1, total)]
+        if total <= 32:
+            for j in range(1, total):
+                acc = acc + gram[it, lax.rem(j + 2 * total - line - 1, total)]
         else:
-            acc = lax.fori_loop(1, n, lambda j, a: a + gram[it, lax.rem(j + 2 * n - r - 1, n)], acc)
+            acc = lax.fori_loop(1, total, lambda j, a: a + gram[it, lax.rem(j + 2 * total - line - 1, total)], acc)
         return jnp.concatenate(
             [acc[:, i * columns : (i + 1) * columns] for i in range(block.shape[0] // group)], axis=0
         )
@@ -247,8 +270,7 @@
     small[4].wait()
     own = own_product(0, OUT_SLAB0, OUT_BAND0)
     both = [jnp.concatenate([probe_tiles[t], own[t]], axis=0) for t in range(per)]
-    block = sum(dot(x, x, MT) for x in both)
-    block = gram_total(0, block)
+    block = gram_total(0, GRAM0, gram_block(both, both))
     squares, cross = block[:count, :count], block[:count, count:]
     cross_t, mapped_sq = block[count:, :count], block[count:, count:]
     step0, squares_inv = eliminate([((cross + cross_t) * 0.5, squares), (squares, eye)])
@@ -267,7 +289,7 @@
     row_products(1)
     send_band(1, OUT_BAND1)
     own1 = own_product(1, OUT_SLAB1, OUT_BAND1)
-    cross = gram_total(1, sum(dot(direction[t], own1[t], MT) for t in range(per)))
+    cross = gram_total(1, GRAM1, gram_block(direction, own1))
     (step1,) = eliminate([((cross + cross.T) * 0.5, renewed)])
     step1_t = step1.T
     for t in range(per):
@@ -287,14 +309,12 @@
         (SLAB0, slab.at[0, pl.ds(0, n - 1)]),
         (OUT_SLAB0, in_slab.at[0]),
         (OUT_BAND0, in_band.at[0]),
-        (GRAM0, gram.at[0, pl.ds(0, n - 1)]),
-        (PAIR0, pair_block.at[0, 1]),
+        (GRAM0, gram.at[0, pl.ds(0, total - 1)]),
         (BAND1, band.at[1, half]),
         (SLAB1, slab.at[1, pl.ds(0, n - 1)]),
         (OUT_SLAB1, in_slab.at[1]),
         (OUT_BAND1, in_band.at[1]),
-        (GRAM1, gram.at[1, pl.ds(0, n - 1)]),
-        (PAIR1, pair_block.at[1, 1]),
+        (GRAM1, gram.at[1, pl.ds(0, total - 1)]),
     ):
         await_ref(send.at[family], ref)
     for copy in out:
@@ -332,13 +352,12 @@
             pltpu.VMEM((2, n - 1, per, count, edge), BF16),
             pltpu.VMEM((2, 2, per, count, edge), F32),
             pltpu.VMEM((2, per, count, edge), F32),
-            pltpu.VMEM((2, n, 8, 128), F32),
-            pltpu.VMEM((2, 2, 8, 128), F32),
+            pltpu.VMEM((2, 2 * n, 8, 128), F32),
             pltpu.SemaphoreType.DMA((chunks,)),
             pltpu.SemaphoreType.DMA((5,)),
             pltpu.SemaphoreType.DMA,
-            pltpu.SemaphoreType.DMA((12,)),
-            pltpu.SemaphoreType.DMA((12,)),
+            pltpu.SemaphoreType.DMA((10,)),
+            pltpu.SemaphoreType.DMA((10,)),
         ]
         return pl.pallas_call(
             functools.partial(kernel, n, chunks),

time: 40.9 us -> 39.9 us (0.976)
  Pallas kernels: 37.2 us -> 36.2 us
    pallas_call x1, Pallas kernels: 37.2 us -> 36.2 us  [local(): pl.pallas_call(functools.partial(kernel, n, chunks), out_shape=(jax.Shape...]
where the time goes in v5:
time: 39.9 us; the launch traced here: 39.6 us
  Pallas kernels  36.2 us (91%)
  local copies, waits for them, and re-layouts  2.75 us (7%)
  between operations  0.64 us (2%)
    pallas_call x1, Pallas kernels, local(): pl.pallas_call(functools.partial(kernel, n, chunks), out_shape=(jax.Shape...  36.2 us
    unnamed x2, local copies, waits for them, and re-layouts  2.75 us

profile of v5, /device:TPU:0, one launch (start us, length us, event | category | flops | bytes accessed | tf_op | source)
XLA Modules:
  0.0 39.6 jit_solution(3979191232517274151)
XLA Ops:
  0.6 36.2 %shard_map.77 = (f32[16,512]{1,0:T(8,128)}, f32[16,512]{1,0:T(8,128)}) custom-call(f32[16,512]{1,0:T(8,128)} %probes_hbm.1, bf16[32,256,256]{2,1,0:T(8,128)(2,1)} %tiles_hbm.1, s32[32]{0:T(128)} %rows_hbm.1, s32[32]{0:T(128)} %cols_hbm.1, s32[32]{0:T(128)} %cnt_hbm.1, bf16[2,256,256]{2,1,0:T(8,128)(2,1)} %diag_hbm.1), custom_call_target="tpu_custom_call" | custom-call | tf_op jit(solution)/shard_map/pallas_call | solution.py:362
  36.9 1.4 %copy.10 = f32[16,512]{1,0:T(8,128)} copy(f32[16,512]{1,0:T(8,128)} %get-tuple-element.4) | data formatting | bytes 65536
  38.2 1.4 %copy.11 = f32[16,512]{1,0:T(8,128)} copy(f32[16,512]{1,0:T(8,128)} %get-tuple-element.5) | data formatting | bytes 65536

commit v6 on v2

--- a/solution.py
+++ b/solution.py
@@ -44,6 +44,23 @@
 def split(x):
     hi = x.astype(BF16)
     return hi, (x - hi.astype(F32)).astype(BF16)
+
+
+def gram_block(lefts, rights):
+    rows = lefts[0].shape[0]
+
+    def thirds(x):
+        hi = x.astype(BF16)
+        rest = x - hi.astype(F32)
+        mid = rest.astype(BF16)
+        low = (rest - mid.astype(F32)).astype(BF16)
+        return jnp.concatenate([hi, mid, low], axis=0)
+
+    left = [thirds(x) for x in lefts]
+    right = left if rights is lefts else [thirds(x) for x in rights]
+    full = sum(fast_dot(a, b, MT) for a, b in zip(left, right))
+    full = full[2 * rows :] + full[rows : 2 * rows] + full[:rows]
+    return full[:, 2 * rows :] + full[:, rows : 2 * rows] + full[:, :rows]
 
 
 def eliminate(pairs):
@@ -153,8 +170,6 @@
     half = pl.ds(c * per, per)
     start(HI_BAND, band_hi.at[half], band_hi.at[half], partner)
     to_slab(HI_SLAB, lambda k: slab_hi.at[n - 1], slab_hi)
-    start(LO_BAND, band_lo.at[half], band_lo.at[half], partner)
-    to_slab(LO_SLAB, lambda k: slab_lo.at[n - 1], slab_lo)
     to_smem.wait()
 
     lane = lax.broadcasted_iota(jnp.int32, (count, edge), 1)
@@ -239,6 +254,8 @@
         fetches[i].wait()
         column_products(i * part, (i + 1) * part, lambda b: band_hi[b])
     send_slab(0, OUT_SLAB0)
+    start(LO_BAND, band_lo.at[half], band_lo.at[half], partner)
+    to_slab(LO_SLAB, lambda k: slab_lo.at[n - 1], slab_lo)
     await_ref(recv.at[HI_SLAB], slab_hi.at[pl.ds(0, n - 1)])
     row_products(lambda s, t: slab_hi[s, t])
     send_band(0, OUT_BAND0)
@@ -246,7 +263,7 @@
     own = own_product(0, lambda t: slab_hi[n - 1, t], OUT_SLAB0, OUT_BAND0)
     probe_tiles = [probes[:, t * edge : (t + 1) * edge] for t in range(per)]
     both = [jnp.concatenate([probe_tiles[t], own[t]], axis=0) for t in range(per)]
-    block = sum(dot(x, x, MT) for x in both)
+    block = gram_block(both, both)
     width = 2 * count
     group = 8
     for i in range(width // group):

time: 39.8 us -> 38.8 us (0.975)
  Pallas kernels: 36.1 us -> 35.2 us
    pallas_call x1, Pallas kernels: 36.1 us -> 35.2 us  [local(): pl.pallas_call(functools.partial(kernel, n, chunks), out_shape=(jax.Shape...]
where the time goes in v6:
time: 38.8 us; the launch traced here: 38.5 us
  Pallas kernels  35.2 us (91%)
  local copies, waits for them, and re-layouts  2.75 us (7%)
  between operations  0.64 us (2%)
    pallas_call x1, Pallas kernels, local(): pl.pallas_call(functools.partial(kernel, n, chunks), out_shape=(jax.Shape...  35.2 us
    unnamed x2, local copies, waits for them, and re-layouts  2.75 us

profile of v6, /device:TPU:0, one launch (start us, length us, event | category | flops | bytes accessed | tf_op | source)
XLA Modules:
  0.0 38.5 jit_solution(12969383132211864095)
XLA Ops:
  0.6 35.2 %shard_map.77 = (f32[16,512]{1,0:T(8,128)}, f32[16,512]{1,0:T(8,128)}) custom-call(f32[16,512]{1,0:T(8,128)} %probes_hbm.1, bf16[32,256,256]{2,1,0:T(8,128)(2,1)} %tiles_hbm.1, s32[32]{0:T(128)} %rows_hbm.1, s32[32]{0:T(128)} %cols_hbm.1, s32[32]{0:T(128)} %cnt_hbm.1, bf16[2,256,256]{2,1,0:T(8,128)(2,1)} %diag_hbm.1), custom_call_target="tpu_custom_call" | custom-call | tf_op jit(solution)/shard_map/pallas_call | solution.py:416
  35.8 1.4 %copy.10 = f32[16,512]{1,0:T(8,128)} copy(f32[16,512]{1,0:T(8,128)} %get-tuple-element.4) | data formatting | bytes 65536
  37.2 1.4 %copy.11 = f32[16,512]{1,0:T(8,128)} copy(f32[16,512]{1,0:T(8,128)} %get-tuple-element.5) | data formatting | bytes 65536
